TPU v7x, 32 devices: a whole 2x2x4 slice. The times are simulated.
32 devices in a mesh: runs: 8 (over z, x), chan: 4 (over y, core).
Axes of the slice: x: 2, y: 2, z: 4, core: 2. Of those that a mesh axis runs over, the one named last changes fastest.
Arguments:
- slices: bfloat16 [64, 512, 8192], P('runs', None, 'chan'), may hold values from -6 to 6
- spectra: bfloat16 [2, 48, 8192], P(None, None, 'chan'), may hold values from -0.0625 to 0.0625
- loadings: float32 [64, 48], replicated, may hold values from 0.5 to 2
- mixing: float32 [2, 48, 48], replicated, may hold values from -1 to 3.5
- halves: int32 [64], replicated, may hold values from 0 to 1, as said below
- partner: int32 [64], replicated, may hold values from 0 to 63, as said below
Outputs:
- new_spectra: float32 [2, 48, 8192], P(None, None, 'chan')
- held_residual: float32 [64, 48, 8192], P('runs', None, 'chan')
Inputs may be any that keep to these rules, and one draw needn't show every extreme that they name: `halves`: exactly half of the 64 runs are in each half. partner pairs every run with a run of the other half, and the partner of a run's partner is the run itself.
All inputs are finite; a program needn't handle non-finite values.
Results may differ from a plain program's by a relative error of at most 0.0045.
Values may be sent and summed in bfloat16 or wider, within the bound.
A program may use at most 64 MiB of HBM per device.

v0:
```python
import jax
import jax.numpy as jnp
from jax import lax
from jax.sharding import PartitionSpec as P

NS_STEPS = 10


def polar_scale(gram):
    eye_rank = jnp.eye(gram.shape[-1], dtype=jnp.float32)
    traces = jnp.trace(gram, axis1=1, axis2=2)
    start = eye_rank[None] / jnp.sqrt(traces + 1e-06)[:, None, None]

    def advance(step, factor):
        left = jnp.einsum("nrs,nrt->nst", factor, gram, precision=lax.Precision.HIGHEST)
        inner = jnp.einsum("nst,ntu->nsu", left, factor, precision=lax.Precision.HIGHEST)
        return 0.5 * jnp.einsum(
            "nrs,nsu->nru", factor, 3.0 * eye_rank[None] - inner, precision=lax.Precision.HIGHEST
        )

    return lax.fori_loop(0, NS_STEPS, advance, start)


def project(slices, rows_low, mixed):
    partial_basis = jnp.einsum("nrj,nij->nri", rows_low, slices, preferred_element_type=jnp.float32)
    basis = lax.psum(partial_basis, "chan")
    scaled = jnp.einsum("nrs,nsi->nri", mixed, basis, precision=lax.Precision.HIGHEST)
    gram = jnp.einsum("nri,nsi->nrs", scaled, scaled, precision=lax.Precision.HIGHEST)
    factor = polar_scale(gram)
    rotated = jnp.einsum("nrs,nri->nsi", factor, scaled, precision=lax.Precision.HIGHEST).astype(
        jnp.bfloat16
    )
    result = jnp.einsum("nsi,nij->nsj", rotated, slices, preferred_element_type=jnp.float32)
    return result


def solve_one(lower, target):
    return jax.scipy.linalg.cho_solve((lower, True), target)


def solve_halves(system, moments):
    lower = jnp.linalg.cholesky(system)
    return jax.vmap(solve_one)(lower, moments)


def body(slices, spectra, loadings, mixing, halves, partner):
    run_count = slices.shape[0]
    total_runs = loadings.shape[0]
    first_run = lax.axis_index("runs") * run_count
    mine = first_run + jnp.arange(run_count, dtype=jnp.int32)
    all_runs = jnp.arange(total_runs, dtype=jnp.int32)
    matches = all_runs[None, :] == mine[:, None]
    my_halves = jnp.sum(jnp.where(matches, halves[None, :], 0), axis=1)
    my_mates = jnp.sum(jnp.where(matches, partner[None, :], 0), axis=1)
    my_loads = jnp.dot(matches.astype(jnp.float32), loadings, precision=lax.Precision.HIGHEST)
    mate_match = (all_runs[None, :] == my_mates[:, None]).astype(jnp.float32)
    mate_loads = jnp.dot(mate_match, loadings, precision=lax.Precision.HIGHEST)
    first_half = (my_halves == 0)[:, None, None]
    own_rows = jnp.where(first_half, spectra[0][None], spectra[1][None])
    own_mix = jnp.where(first_half, mixing[0][None], mixing[1][None]) * my_loads[:, None, :]
    projected = project(slices, own_rows, own_mix)
    terms = jnp.einsum("nsr,nsj->nrj", own_mix, projected, precision=lax.Precision.HIGHEST)
    mine_member = (my_halves[:, None] == jnp.arange(2, dtype=jnp.int32)[None, :]).astype(
        jnp.float32
    )
    partial_moments = jnp.einsum("nh,nrj->hrj", mine_member, terms, precision=lax.Precision.HIGHEST)
    member = (halves[:, None] == jnp.arange(2, dtype=jnp.int32)[None, :]).astype(jnp.float32)
    cross = jnp.einsum("kh,kr,ks->hrs", member, loadings, loadings, precision=lax.Precision.HIGHEST)
    inner_mix = jnp.einsum("hsr,hst->hrt", mixing, mixing, precision=lax.Precision.HIGHEST)
    system = inner_mix * cross
    moments = lax.psum(partial_moments, "runs")
    new_spectra = solve_halves(system, moments)
    held_rows = jnp.where(first_half, new_spectra[1][None], new_spectra[0][None])
    held_mix = jnp.where(first_half, mixing[1][None], mixing[0][None]) * mate_loads[:, None, :]
    held_projected = project(slices, held_rows.astype(jnp.bfloat16), held_mix)
    model_part = jnp.einsum("nrs,nsj->nrj", held_mix, held_rows, precision=lax.Precision.HIGHEST)
    return (new_spectra, held_projected - model_part)


def solution(mesh):
    placed = (P("runs", None, "chan"), P(None, None, "chan"), P(), P(), P(), P())
    return jax.shard_map(
        body,
        mesh=mesh,
        in_specs=placed,
        out_specs=(P(None, None, "chan"), P("runs", None, "chan")),
        check_vma=False,
    )
```

profile of v0, /device:TPU:11, one launch (start us, length us, event | category | flops | bytes accessed | tf_op | source)
XLA Modules:
  0.0 245.6 jit_solution(7506214992397148198)
XLA Ops:
  7.2 0.9 select_reduce_fusion.3
  8.1 1.1 slice_bitcast_fusion.3
  9.2 11.8 %fusion.17 = f32[8,48,512]{2,1,0:T(8,128)} fusion(bf16[8,512,2048]{2,1,0:T(8,128)(2,1)} %param.10, pred[8]{0:T(512)(128)(4,1)S(1)} %broadcast_compare_fusion, bf16[48,2048]{1,0:T(8,128)(2,1)S(1)} %get-tuple-element.81, bf16[48,2048]{1,0:T(8,128)(2,1)S(1)} %get-tuple-element.80), kind=kOutput, calls=%fused_computation.23 | convolution fusion | flops 806092800 | bytes 17956872 | tf_op jit(solution)/shard_map/nrj,nij->nri/dot_general | solution.py:25
  22.1 34.0 %all-reduce.4.cloned.1.call-done = f32[8,48,512]{2,1,0:T(8,128)} async-done(((f32[8,48,512]{2,1,0:T(8,128)}), f32[8,48,512]{2,1,0:T(8,128)}) %all-reduce.4.cloned.1.call-update) | async-done | bytes 786448 | tf_op jit(solution)/shard_map/psum | solution.py:26
  56.1 2.0 fusion.26
  58.1 0.9 select_reduce_fusion.1
  59.1 11.6 %while.22 = (s32[]{:T(128)}, f32[8,48,48]{1,2,0:T(8,128)S(1)}, f32[8,48,48]{2,1,0:T(8,128)S(1)}, s32[]{:T(128)}) while((s32[]{:T(128)}, f32[8,48,48]{1,2,0:T(8,128)S(1)}, f32[8,48,48]{2,1,0:T(8,128)S(1)}, s32[]{:T(128)}) %tuple.47), condition=%wide.region_6.7_spmd.clone, body=%wide.region_5.6_spmd.clone.sunk | while | flops 31891968 | bytes 829493 | solution.py:21
  60.8 0.4 convolution_subtract_fusion.5
  65.4 0.4 convolution_subtract_fusion.5
  66.6 0.4 convolution_subtract_fusion.5
  67.7 0.4 convolution_subtract_fusion.5
  70.8 0.8 convolution_convert_fusion.1
  71.6 8.8 %fusion.66 = f32[8,48,2048]{2,1,0:T(8,128)S(1)} fusion(bf16[8,48,512]{2,1,0:T(8,128)(2,1)S(1)} %convolution_convert_fusion.1, bf16[8,512,2048]{2,1,0:T(8,128)(2,1)} %param.10), kind=kOutput, calls=%fused_computation.102 | convolution fusion | flops 805306368 | bytes 20316160 | tf_op jit(solution)/shard_map/nsi,nij->nsj/dot_general | solution.py:33
  80.4 3.1 %fusion.25 = f32[8,48,2048]{2,1,0:T(8,128)S(1)} fusion(f32[8,48,2048]{2,1,0:T(8,128)S(1)} %fusion.66, f32[8,48]{1,0:T(8,128)S(1)} %fusion.56, f32[48,48]{1,0:T(8,128)S(1)} %get-tuple-element.83, f32[48,48]{1,0:T(8,128)S(1)} %get-tuple-element.82, pred[8]{0:T(512)(128)(4,1)S(1)} %broadcast_compare_fusion), kind=kOutput, calls=%fused_computation.41 | convolution fusion | flops 453021696 | bytes 6311432 | tf_op jit(solution)/shard_map/nsr,nsj->nrj/dot_general | solution.py:62
  83.4 3.3 %fusion.10 = f32[2,48,2048]{2,0,1:T(2,128)S(1)} fusion(f32[8,48,2048]{2,1,0:T(8,128)S(1)} %fusion.25, s32[8]{0:T(128)S(1)} %get-tuple-element.65), kind=kOutput, calls=%fused_computation.15 | convolution fusion | flops 18874384 | bytes 3932192 | tf_op jit(solution)/shard_map/nh,nrj->hrj/dot_general | solution.py:66
  86.8 1.3 copy.24
  88.2 9.0 %custom-call.11 = f32[2,48,48]{2,1,0:T(8,128)S(1)} custom-call(f32[2,48,48]{2,1,0:T(8,128)S(1)} %fusion.48), custom_call_target="Cholesky" | custom-call | tf_op jit(solution)/shard_map/jit(cholesky)/cholesky | solution.py:42
  97.5 7.4 %custom-call.12 = f32[2,1,48,48]{2,3,1,0:T(8,128)S(1)} custom-call(f32[2,1,48,48]{3,2,1,0:T(8,128)S(1)} %select_bitcast_fusion), custom_call_target="InvertDiagBlocksLowerTriangular" | custom-call | tf_op jit(solution)/shard_map/vmap(jit(_cho_solve))/triangular_solve | solution.py:38
  104.9 57.1 %all-reduce.6.cloned.1.call-done = f32[2,48,2048]{2,1,0:T(8,128)} async-done(((f32[2,48,2048]{2,1,0:T(8,128)}), f32[2,48,2048]{2,1,0:T(8,128)}) %all-reduce.6.cloned.1.call-update) | async-done | bytes 786448 | tf_op jit(solution)/shard_map/psum | solution.py:71
  162.0 2.0 fusion.45
  163.9 0.8 fusion.43
  164.8 12.1 %fusion.12 = f32[8,48,512]{2,1,0:T(8,128)} fusion(bf16[8,512,2048]{2,1,0:T(8,128)(2,1)} %param.10, f32[48,2048]{1,0:T(8,128)S(1)} %get-tuple-element.79, f32[48,2048]{1,0:T(8,128)S(1)} %get-tuple-element.78, pred[8]{0:T(512)(128)(4,1)S(1)} %broadcast_compare_fusion), kind=kOutput, calls=%fused_computation.18 | convolution fusion | flops 806092800 | bytes 18350088 | tf_op jit(solution)/shard_map/nrj,nij->nri/dot_general | solution.py:25
  177.1 4.5 %fusion.8 = f32[8,48,2048]{2,1,0:T(8,128)} fusion(f32[48,2048]{1,0:T(8,128)S(1)} %get-tuple-element.79, f32[48,2048]{1,0:T(8,128)S(1)} %get-tuple-element.78, pred[8]{0:T(512)(128)(4,1)S(1)} %broadcast_compare_fusion, f32[8,48]{1,0:T(8,128)S(1)} %fusion.59, f32[48,48]{1,0:T(8,128)S(1)} %get-tuple-element.83, f32[48,48]{1,0:T(8,128)S(1)} %get-tuple-element.82), kind=kOutput, calls=%fused_computation.12 | convolution fusion | flops 453808128 | bytes 3952136 | tf_op jit(solution)/shard_map/nrs,nsj->nrj/dot_general | solution.py:76
  181.6 30.5 %all-reduce.8.cloned.1.call-done = f32[8,48,512]{2,1,0:T(8,128)} async-done(((f32[8,48,512]{2,1,0:T(8,128)}), f32[8,48,512]{2,1,0:T(8,128)}) %all-reduce.8.cloned.1.call-update) | async-done | bytes 786448 | tf_op jit(solution)/shard_map/psum | solution.py:26
  212.1 2.0 fusion.24
  214.0 0.9 select_reduce_fusion
  215.1 11.7 %while.23 = (s32[]{:T(128)}, f32[8,48,48]{1,2,0:T(8,128)S(1)}, f32[8,48,48]{2,1,0:T(8,128)S(1)}, s32[]{:T(128)}) while((s32[]{:T(128)}, f32[8,48,48]{1,2,0:T(8,128)S(1)}, f32[8,48,48]{2,1,0:T(8,128)S(1)}, s32[]{:T(128)}) %tuple.50), condition=%wide.region_12.13_spmd.clone, body=%wide.region_11.12_spmd.clone.sunk | while | flops 31891968 | bytes 829493 | solution.py:21
  217.8 0.4 convolution_subtract_fusion.6
  218.9 0.4 convolution_subtract_fusion.6
  220.0 0.4 convolution_subtract_fusion.6
  226.8 0.8 convolution_convert_fusion
  227.6 11.5 %convolution_subtract_fusion.2 = f32[8,48,2048]{2,1,0:T(8,128)} fusion(f32[8,48,2048]{2,1,0:T(8,128)} %fusion.8, bf16[8,48,512]{2,1,0:T(8,128)(2,1)S(1)} %convolution_convert_fusion, bf16[8,512,2048]{2,1,0:T(8,128)(2,1)} %param.10), kind=kOutput, calls=%fused_computation.17 | convolution fusion | flops 806092800 | bytes 23461888 | tf_op jit(solution)/shard_map/nsi,nij->nsj/dot_general | solution.py:33
  (130 shorter events, 20.6 us)
Async XLA Ops:
  7.2 49.0 %all-reduce.4.cloned.1.call-start = ((), (), s32[]{:S(2)}) async-start(), calls=%async_computation | async-start | bytes 1572864 | tf_op jit(solution)/shard_map/psum | solution.py:26
  9.2 12.0 %copy-start.3 = (s32[64]{0:T(128)S(1)}, s32[64]{0:T(128)}, u32[]{:S(2)}) copy-start(s32[64]{0:T(128)} %param.14) | copy-start | bytes 772
  9.2 12.0 %copy-start.2 = (f32[64,48]{0,1:T(8,128)S(1)}, f32[64,48]{0,1:T(8,128)}, u32[]{:S(2)}) copy-start(f32[64,48]{0,1:T(8,128)} %param.12) | copy-start | bytes 36868
  9.2 12.4 %copy-start.1 = (f32[2,48,48]{2,1,0:T(8,128)S(1)}, f32[2,48,48]{2,1,0:T(8,128)}, u32[]{:S(2)}) copy-start(f32[2,48,48]{2,1,0:T(8,128)} %param.13) | copy-start | bytes 55300
  21.1 140.9 %all-reduce.6.cloned.1.call-start = ((), (), s32[]{:S(2)}) async-start(), calls=%async_computation.1 | async-start | bytes 1572864 | tf_op jit(solution)/shard_map/psum | solution.py:71
  88.2 123.9 %all-reduce.8.cloned.1.call-start = ((), (), s32[]{:S(2)}) async-start(), calls=%async_computation.2 | async-start | bytes 1572864 | tf_op jit(solution)/shard_map/psum | solution.py:26
  164.8 12.1 %copy-start = (f32[2,48,2048]{2,1,0:T(8,128)}, f32[2,48,2048]{2,1,0:T(8,128)S(1)}, u32[]{:S(2)}) copy-start(f32[2,48,2048]{2,1,0:T(8,128)S(1)} %fusion.43) | copy-start | bytes 2359300
Sparse Core Ops, SparseCore 0:
  21.2 34.8 all-reduce.3
  88.3 73.6 all-reduce.5
  177.0 34.9 all-reduce.7
where the time goes:
time: 248 us; the launch traced here: 246 us
  waiting for transfers between devices  122 us (49%)
  matrix products  87.4 us (35%)
  other arithmetic  17.9 us (7%)
  between operations  14 us (6%)
  local copies, waits for them, and re-layouts  3 us (1%)
    psum x2, waiting for transfers between devices, project(): basis = lax.psum(partial_basis, 'chan')  64.5 us
    psum x1, waiting for transfers between devices, body(): moments = lax.psum(partial_moments, 'runs')  57.1 us
    dot_general x2, matrix products, project(): jnp.einsum('nrj,nij->nri', rows_low, slices, preferred_element_type=jnp.f...  23.9 us
    dot_general x2, matrix products, project(): jnp.einsum('nsi,nij->nsj', rotated, slices, preferred_element_type=jnp.fl...  20.3 us
    another operation x4, other arithmetic, solve_halves(): lower = jnp.linalg.cholesky(system)  9.18 us
    dot_general x20, matrix products, advance(): jnp.einsum('nst,ntu->nsu', left, factor, precision=lax.Precision.HIGHEST)  8.68 us
    another operation x3, other arithmetic, solve_one(): return jax.scipy.linalg.cho_solve((lower, True), target)  7.47 us
    dot_general x20, matrix products, advance(): jnp.einsum('nrs,nrt->nst', factor, gram, precision=lax.Precision.HIGHEST)  6.4 us
  transfers between devices with their start and end apart: 3, of which 3 were waited for; matrix products, arithmetic and copies ran while one was open for 9% of the time, Pallas kernels for 0%

commit v1 on v0

v1 whole, which is shorter than its diff:
```python
import functools

import jax
import jax.numpy as jnp
from jax import lax
from jax.experimental import pallas as pl
from jax.experimental.pallas import tpu as pltpu
from jax.sharding import PartitionSpec as P

NS_STEPS = 10
HI = lax.Precision.HIGHEST
F32 = jnp.float32
BF16 = jnp.bfloat16
NT = (((1,), (1,)), ((), ()))
MESH = pl.DeviceIdType.MESH


def mul(a, b):
    return jnp.dot(a, b, precision=HI, preferred_element_type=F32)


def identity(size):
    rows = lax.broadcasted_iota(jnp.int32, (size, size), 0)
    cols = lax.broadcasted_iota(jnp.int32, (size, size), 1)
    return (rows == cols).astype(F32)


def polar_rotate(mixes, bases):
    rank = mixes[0].shape[0]
    eye = identity(rank)
    scaled = [mul(m, b) for m, b in zip(mixes, bases)]
    grams = [lax.dot_general(s, s, NT, precision=HI, preferred_element_type=F32) for s in scaled]
    traces = [jnp.sum(jnp.sum(g * eye, axis=1, keepdims=True), axis=0, keepdims=True) + 1e-06 for g in grams]
    ys = [g / t for g, t in zip(grams, traces)]
    xs = [eye * lax.rsqrt(t) for t in traces]
    for step in range(NS_STEPS):
        zs = [1.5 * eye - 0.5 * y for y in ys]
        if step == 0:
            xs = [z * lax.rsqrt(t) for z, t in zip(zs, traces)]
        else:
            xs = [mul(x, z) for x, z in zip(xs, zs)]
        if step < NS_STEPS - 1:
            ws = [mul(y, z) for y, z in zip(ys, zs)]
            ys = [mul(w, z) for w, z in zip(ws, zs)]
    return [mul(x, s) for x, s in zip(xs, scaled)]


def invert_pair(systems):
    rank = systems[0].shape[0]
    eye = identity(rank)
    lane = lax.broadcasted_iota(jnp.int32, (rank, 2 * rank), 1)
    sub = lax.broadcasted_iota(jnp.int32, (rank, 2 * rank), 0)

    def step(j, tables):
        out = []
        for t in tables:
            col = jnp.sum(jnp.where(lane == j, t, 0.0), axis=1, keepdims=True)
            row = jnp.sum(jnp.where(sub == j, t, 0.0), axis=0, keepdims=True)
            pivot = jnp.sum(jnp.where(sub[:, :1] == j, col, 0.0), axis=0, keepdims=True)
            scaled = row / pivot
            out.append(jnp.where(sub == j, scaled, t - col * scaled))
        return out

    tables = [jnp.concatenate([a, eye], axis=1) for a in systems]
    tables = lax.fori_loop(0, rank, step, tables)
    return [t[:, rank:] for t in tables]


def kernel(
    n, sl, sp, omix, hmix, hf, sysm, new_o, res_o,
    s, bs1, br1, own1, gb, psend, p32, rrecv, fitb, rows, gcat, bs2, br2, own2, rot,
    dsem, s1s, s1r, s2s, s2r, s3s, s3r, s4s, s4r, s5s, s5r, s6s, s6r,
):
    c = lax.axis_index("chan")
    r = lax.axis_index("runs")
    count, times, width = sl.shape
    rank = omix.shape[1]
    per = count // 4
    blocks = n // 2
    w = width // blocks
    peers = [(c + 2) % 4, 3 - c, c + 1 - 2 * (c % 2)]
    order = [p * per + i for p in peers + [c] for i in range(per)]

    def rows_of(k):
        return pl.ds(pl.multiple_of(k * times, times), times)

    loads = []
    for t, k in enumerate(order):
        load = pltpu.make_async_copy(sl.at[k], s.at[rows_of(k)], dsem.at[t])
        load.start()
        loads.append(load)

    barrier = pltpu.get_barrier_semaphore()
    for p in peers:
        pl.semaphore_signal(barrier, inc=1, device_id={"chan": p}, device_id_type=MESH)
    for d in range(1, n):
        pl.semaphore_signal(barrier, inc=1, device_id={"runs": (r + d) % n}, device_id_type=MESH)
    pl.semaphore_wait(barrier, 3 + n - 1)

    def remote(src, dst, ssem, rsem, where):
        return pltpu.make_async_remote_copy(
            src_ref=src, dst_ref=dst, send_sem=ssem, recv_sem=rsem, device_id=where, device_id_type=MESH
        )

    def basis_phase(both, flip, bs, br, own, ssem, rsem, waits):
        sends = []
        for t, k in enumerate(order):
            if waits:
                loads[t].wait()
            part = lax.dot_general(s[rows_of(k)], both, NT, preferred_element_type=F32).T
            h = hf[k]
            if flip:
                h = 1.0 - h
            chosen = part[:rank] * (1.0 - h) + part[rank:] * h
            q, i = t // per, t % per
            if q < 3:
                bs[k] = chosen.astype(BF16)
                if i == per - 1:
                    p = peers[q]
                    send = remote(
                        bs.at[pl.ds(p * per, per)], br.at[c], ssem.at[q], rsem.at[c], {"chan": p}
                    )
                    send.start()
                    sends.append(send)
            else:
                own[i] = chosen
        return sends

    def basis_sum(bs, br, own, ssem, rsem):
        for q, p in enumerate(peers):
            remote(
                bs.at[pl.ds(p * per, per)], br.at[p], ssem.at[q], rsem.at[p], {"chan": p}
            ).wait_recv()
        return [
            own[i] + br[peers[0], i].astype(F32) + br[peers[1], i].astype(F32) + br[peers[2], i].astype(F32)
            for i in range(per)
        ]

    def share(buf, ssem, rsem):
        mine = buf.at[pl.ds(c * per, per)]
        sends = []
        for q, p in enumerate(peers):
            send = remote(mine, mine, ssem.at[q], rsem.at[c], {"chan": p})
            send.start()
            sends.append(send)
        return sends

    def shared(buf, ssem, rsem):
        for q, p in enumerate(peers):
            theirs = buf.at[pl.ds(p * per, per)]
            remote(theirs, theirs, ssem.at[q], rsem.at[p], {"chan": p}).wait_recv()

    sends = basis_phase(sp[...], False, bs1, br1, own1, s1s, s1r, True)
    inverses = invert_pair([sysm[0], sysm[1]])
    backs = []
    for i in range(per):
        h = hf[c * per + i]
        chosen = inverses[0] * (1.0 - h) + inverses[1] * h
        backs.append(
            lax.dot_general(chosen, omix[c * per + i], NT, precision=HI, preferred_element_type=F32)
        )
    bases = basis_sum(bs1, br1, own1, s1s, s1r)
    rotated = polar_rotate([omix[c * per + i] for i in range(per)], bases)
    for i in range(per):
        low = rotated[i].astype(BF16).astype(F32)
        gb[c * per + i] = mul(backs[i], low).astype(BF16)
    sends += share(gb, s2s, s2r)
    shared(gb, s2s, s2r)
    for k in range(count):
        h = hf[k]
        g = gb[k].astype(F32)
        gcat[:rank, k * times : (k + 1) * times] = (g * (1.0 - h)).astype(BF16)
        gcat[rank:, k * times : (k + 1) * times] = (g * h).astype(BF16)

    def chunk(block):
        cols = pl.ds(pl.multiple_of(block * w, w), w)
        return jnp.dot(gcat[...], s[:, cols], preferred_element_type=F32)

    def send_chunk(j, d):
        send = remote(psend.at[j], rrecv.at[r], s3s.at[d], s3r.at[r], {"runs": j})
        send.start()
        sends.append(send)

    count_sent = 0
    for step in range(1, blocks):
        block = (r + step) % blocks
        part = chunk(block)
        for half in range(2):
            j = half * blocks + block
            psend[j] = part[half * rank : (half + 1) * rank].astype(BF16)
            send_chunk(j, count_sent)
            count_sent += 1
    part = chunk(r % blocks)
    p32[0] = part[:rank]
    p32[1] = part[rank:]
    j = (r + blocks) % n
    psend[j] = p32[1 - r // blocks].astype(BF16)
    send_chunk(j, count_sent)
    total = p32[r // blocks]
    for d in range(1, n):
        j = (r + d) % n
        remote(psend.at[j], rrecv.at[j], s3s.at[d - 1], s3r.at[j], {"runs": j}).wait_recv()
        total = total + rrecv[j].astype(F32)
    fitb[r] = total.astype(BF16)
    for d in range(1, n):
        send = remote(fitb.at[r], fitb.at[r], s4s.at[d - 1], s4r.at[r], {"runs": (r + d) % n})
        send.start()
        sends.append(send)
    for d in range(1, n):
        j = (r + d) % n
        remote(fitb.at[j], fitb.at[j], s4s.at[d - 1], s4r.at[j], {"runs": j}).wait_recv()
    for half in range(2):
        for block in range(blocks):
            low = fitb[half * blocks + block]
            rows[half * rank : (half + 1) * rank, block * w : (block + 1) * w] = low
            new_o[half, :, block * w : (block + 1) * w] = low.astype(F32)

    sends += basis_phase(rows[...], True, bs2, br2, own2, s5s, s5r, False)

    def model(k):
        h = hf[k]
        m = hmix[k]
        high = m.astype(BF16).astype(F32)
        parts = [high, m - high]
        left = jnp.concatenate(
            [jnp.concatenate([v * h, v * (1.0 - h)], axis=1) for v in parts], axis=0
        ).astype(BF16)
        both = jnp.dot(left, rows[...], preferred_element_type=F32)
        return both[:rank] + both[rank:]

    for k in range(count):
        res_o[k] = model(k)
    bases = basis_sum(bs2, br2, own2, s5s, s5r)
    rotated = polar_rotate([hmix[c * per + i] for i in range(per)], bases)
    for i in range(per):
        rot[c * per + i] = rotated[i].astype(BF16)
    sends += share(rot, s6s, s6r)
    shared(rot, s6s, s6r)
    for k in range(count):
        res_o[k] = (
            jnp.dot(rot[k], s[k * times : (k + 1) * times], preferred_element_type=F32) - res_o[k]
        )
    for send in sends:
        send.wait_send()


def body(n, slices, spectra, loadings, mixing, halves, partner):
    run_count, times, width = slices.shape
    rank = mixing.shape[-1]
    total_runs = loadings.shape[0]
    first_run = lax.axis_index("runs") * run_count
    mine = first_run + jnp.arange(run_count, dtype=jnp.int32)
    all_runs = jnp.arange(total_runs, dtype=jnp.int32)
    matches = all_runs[None, :] == mine[:, None]
    my_halves = jnp.sum(jnp.where(matches, halves[None, :], 0), axis=1)
    my_mates = jnp.sum(jnp.where(matches, partner[None, :], 0), axis=1)
    my_loads = jnp.dot(matches.astype(F32), loadings, precision=HI)
    mate_match = (all_runs[None, :] == my_mates[:, None]).astype(F32)
    mate_loads = jnp.dot(mate_match, loadings, precision=HI)
    first_half = (my_halves == 0)[:, None, None]
    own_mix = jnp.where(first_half, mixing[0][None], mixing[1][None]) * my_loads[:, None, :]
    held_mix = jnp.where(first_half, mixing[1][None], mixing[0][None]) * mate_loads[:, None, :]
    member = (halves[:, None] == jnp.arange(2, dtype=jnp.int32)[None, :]).astype(F32)
    cross = jnp.einsum("kh,kr,ks->hrs", member, loadings, loadings, precision=HI)
    inner_mix = jnp.einsum("hsr,hst->hrt", mixing, mixing, precision=HI)
    system = inner_mix * cross

    per = run_count // 4
    w = 2 * width // n
    vmem = pl.BlockSpec(memory_space=pltpu.VMEM)
    dma = pltpu.SemaphoreType.DMA
    new_spectra, residual = pl.pallas_call(
        functools.partial(kernel, n),
        out_shape=(
            jax.ShapeDtypeStruct((2, rank, width), F32),
            jax.ShapeDtypeStruct((run_count, rank, width), F32),
        ),
        in_specs=[
            pl.BlockSpec(memory_space=pl.ANY), vmem, vmem, vmem,
            pl.BlockSpec(memory_space=pltpu.SMEM), vmem,
        ],
        out_specs=(vmem, vmem),
        scratch_shapes=[
            pltpu.VMEM((run_count * times, width), BF16),
            pltpu.VMEM((run_count, rank, times), BF16),
            pltpu.VMEM((4, per, rank, times), BF16),
            pltpu.VMEM((per, rank, times), F32),
            pltpu.VMEM((run_count, rank, times), BF16),
            pltpu.VMEM((n, rank, w), BF16),
            pltpu.VMEM((2, rank, w), F32),
            pltpu.VMEM((n, rank, w), BF16),
            pltpu.VMEM((n, rank, w), BF16),
            pltpu.VMEM((2 * rank, width), BF16),
            pltpu.VMEM((2 * rank, run_count * times), BF16),
            pltpu.VMEM((run_count, rank, times), BF16),
            pltpu.VMEM((4, per, rank, times), BF16),
            pltpu.VMEM((per, rank, times), F32),
            pltpu.VMEM((run_count, rank, times), BF16),
            dma((run_count,)),
            dma((3,)), dma((4,)),
            dma((3,)), dma((4,)),
            dma((n - 1,)), dma((n,)),
            dma((n - 1,)), dma((n,)),
            dma((3,)), dma((4,)),
            dma((3,)), dma((4,)),
        ],
        compiler_params=pltpu.CompilerParams(
            collective_id=0, has_side_effects=True, vmem_limit_bytes=56 << 20
        ),
        name="parafac_half",
    )(
        slices, spectra.reshape(2 * rank, width), own_mix, held_mix,
        my_halves.astype(F32), system,
    )
    return (new_spectra, residual)


def solution(mesh):
    placed = (P("runs", None, "chan"), P(None, None, "chan"), P(), P(), P(), P())
    return jax.shard_map(
        functools.partial(body, mesh.shape["runs"]),
        mesh=mesh,
        in_specs=placed,
        out_specs=(P(None, None, "chan"), P("runs", None, "chan")),
        check_vma=False,
    )
```

time: 248 us -> 90.3 us (0.36)
  waiting for transfers between devices: 122 us -> 0 us
  matrix products: 87.4 us -> 4.62 us
  Pallas kernels: 0 us -> 74.8 us
  other arithmetic: 17.9 us -> 2.95 us
  between operations: 14 us -> 0.66 us
  local copies, waits for them, and re-layouts: 3 us -> 6.73 us
    psum x3 -> x0, waiting for transfers between devices: 122 us -> none  [the longest x2 64.5 us: project(): basis = lax.psum(partial_basis, 'chan')]
    dot_general x77 -> x4, matrix products: 84.7 us -> 4.62 us  [the longest x1 1.61 us: body(): jnp.einsum('kh,kr,ks->hrs', member, loadings, loadings, precision=HI)]
    pallas_call x0 -> x1, Pallas kernels: none -> 74.8 us  [body(): pl.pallas_call(functools.partial(kernel, n), out_shape=(jax.ShapeDtypeStr...]
    another operation x8 -> x1, other arithmetic: 16.7 us -> 0.66 us  [the longest x4 9.18 us: solve_halves(): lower = jnp.linalg.cholesky(system)]
    unnamed x8 -> x2, local copies, waits for them, and re-layouts: 0.03 us -> 5.97 us
    another operation x2 -> x0, matrix products: 2.76 us -> none  [solve_one(): return jax.scipy.linalg.cho_solve((lower, True), target)]
  transfers between devices with their start and end apart: 3 -> 0, of which waited for: 3 -> 0; matrix products, arithmetic and copies ran while one was open for 9% -> 0% of each run, Pallas kernels for 0% -> 0%
where the time goes in v1:
time: 90.3 us; the launch traced here: 89.7 us
  Pallas kernels  74.8 us (83%)
  local copies, waits for them, and re-layouts  6.73 us (7%)
  matrix products  4.62 us (5%)
  other arithmetic  2.95 us (3%)
    pallas_call x1, Pallas kernels, body(): pl.pallas_call(functools.partial(kernel, n), out_shape=(jax.ShapeDtypeStr...  74.8 us
    unnamed x2, local copies, waits for them, and re-layouts  5.97 us

profile of v1, /device:TPU:11, one launch (start us, length us, event | category | flops | bytes accessed | tf_op | source)
XLA Modules:
  0.0 89.7 jit_solution(3487055259353880840)
XLA Ops:
  0.6 0.7 compare_convert_fusion
  1.3 0.9 select_reduce_fusion
  2.2 0.6 convert_element_type.2.hf
  2.8 0.9 %fusion.7 = f32[8,48]{1,0:T(8,128)S(1)} fusion(f32[64,48]{0,1:T(8,128)} %param.8, s32[8]{0:T(128)S(1)} %get-tuple-element.2), kind=kOutput, calls=%fused_computation.16 | convolution fusion | flops 295424 | bytes 13856 | tf_op jit(solution)/shard_map/dot_general | solution.py:259
  3.7 0.9 %fusion.6 = f32[8,48]{1,0:T(8,128)S(1)} fusion(f32[64,48]{0,1:T(8,128)} %param.8, s32[8]{0:T(128)S(1)} %iota_add_fusion), kind=kOutput, calls=%fused_computation.15 | convolution fusion | flops 295424 | bytes 13856 | tf_op jit(solution)/shard_map/dot_general | solution.py:257
  4.6 1.2 %fusion.10 = f32[2,48,48]{2,1,0:T(8,128)S(1)} fusion(f32[2,48,48]{2,1,0:T(8,128)} %param.9), kind=kOutput, calls=%fused_computation.22 | convolution fusion | flops 2654208 | bytes 36864 | tf_op jit(solution)/shard_map/hsr,hst->hrt/dot_general | solution.py:265
  5.8 1.6 %fusion.sysm = f32[2,48,48]{2,1,0:T(8,128)} fusion(f32[2,48,48]{2,1,0:T(8,128)S(1)} %fusion.10, f32[64,48]{0,1:T(8,128)} %param.8, f32[64,2]{0,1:T(2,128)S(1)} %compare_convert_fusion), kind=kOutput, calls=%fused_computation.1 | convolution fusion | flops 3549696 | bytes 49664 | tf_op jit(solution)/shard_map/kh,kr,ks->hrs/dot_general | solution.py:264
  7.4 0.8 slice_bitcast_fusion.1
  8.1 0.8 select_multiply_fusion
  9.0 74.8 %parafac_half.1 = (f32[2,48,2048]{2,1,0:T(8,128)}, f32[8,48,2048]{2,1,0:T(8,128)}) custom-call(bf16[8,512,2048]{2,1,0:T(8,128)(2,1)} %sl.1, bf16[96,2048]{1,0:T(8,128)(2,1)} %bitcast.19, f32[8,48,48]{2,1,0:T(8,128)} %get-tuple-element.5.omix, f32[8,48,48]{2,1,0:T(8,128)} %get-tuple-element.4.hmix, f32[8]{0:T(128)} %convert_element_type.2.hf, ...), custom_call_target="tpu_custom_call" | custom-call | tf_op jit(solution)/shard_map/parafac_half/pallas_call | solution.py:272
  83.8 2.1 %copy.13 = f32[2,48,2048]{2,1,0:T(8,128)} copy(f32[2,48,2048]{2,1,0:T(8,128)} %get-tuple-element.10) | data formatting | bytes 1572864
  85.8 3.9 %copy.14 = f32[8,48,2048]{2,1,0:T(8,128)} copy(f32[8,48,2048]{2,1,0:T(8,128)} %get-tuple-element.11) | data formatting | bytes 6291456
  (2 shorter events, 0.0 us)

commit v2 on v1

--- a/solution.py
+++ b/solution.py
@@ -67,7 +67,7 @@
 
 
 def kernel(
-    n, sl, sp, omix, hmix, hf, sysm, new_o, res_o,
+    n, sl, sp, omix, hmix, hf, halves, loadings, mixing, new_o, res_o,
     s, bs1, br1, own1, gb, psend, p32, rrecv, fitb, rows, gcat, bs2, br2, own2, rot,
     dsem, s1s, s1r, s2s, s2r, s3s, s3r, s4s, s4r, s5s, s5r, s6s, s6r,
 ):
@@ -114,7 +114,7 @@
             chosen = part[:rank] * (1.0 - h) + part[rank:] * h
             q, i = t // per, t % per
             if q < 3:
-                bs[k] = chosen.astype(BF16)
+                bs[k] = chosen
                 if i == per - 1:
                     p = peers[q]
                     send = remote(
@@ -132,7 +132,7 @@
                 bs.at[pl.ds(p * per, per)], br.at[p], ssem.at[q], rsem.at[p], {"chan": p}
             ).wait_recv()
         return [
-            own[i] + br[peers[0], i].astype(F32) + br[peers[1], i].astype(F32) + br[peers[2], i].astype(F32)
+            own[i] + br[peers[0], i] + br[peers[1], i] + br[peers[2], i]
             for i in range(per)
         ]
 
@@ -151,7 +151,14 @@
             remote(theirs, theirs, ssem.at[q], rsem.at[p], {"chan": p}).wait_recv()
 
     sends = basis_phase(sp[...], False, bs1, br1, own1, s1s, s1r, True)
-    inverses = invert_pair([sysm[0], sysm[1]])
+    second = halves[...].astype(F32)
+    every = loadings[...]
+    systems = []
+    for half, member in enumerate((1.0 - second, second)):
+        part = (every * member).T
+        mix = mixing[half]
+        systems.append(mul(mix.T, mix) * mul(part, every))
+    inverses = invert_pair(systems)
     backs = []
     for i in range(per):
         h = hf[c * per + i]
@@ -213,7 +220,7 @@
         for block in range(blocks):
             low = fitb[half * blocks + block]
             rows[half * rank : (half + 1) * rank, block * w : (block + 1) * w] = low
-            new_o[half, :, block * w : (block + 1) * w] = low.astype(F32)
+            new_o[half, :, block * w : (block + 1) * w] = low
 
     sends += basis_phase(rows[...], True, bs2, br2, own2, s5s, s5r, False)
 
@@ -260,10 +267,6 @@
     first_half = (my_halves == 0)[:, None, None]
     own_mix = jnp.where(first_half, mixing[0][None], mixing[1][None]) * my_loads[:, None, :]
     held_mix = jnp.where(first_half, mixing[1][None], mixing[0][None]) * mate_loads[:, None, :]
-    member = (halves[:, None] == jnp.arange(2, dtype=jnp.int32)[None, :]).astype(F32)
-    cross = jnp.einsum("kh,kr,ks->hrs", member, loadings, loadings, precision=HI)
-    inner_mix = jnp.einsum("hsr,hst->hrt", mixing, mixing, precision=HI)
-    system = inner_mix * cross
 
     per = run_count // 4
     w = 2 * width // n
@@ -272,18 +275,18 @@
     new_spectra, residual = pl.pallas_call(
         functools.partial(kernel, n),
         out_shape=(
-            jax.ShapeDtypeStruct((2, rank, width), F32),
+            jax.ShapeDtypeStruct((2, rank, width), BF16),
             jax.ShapeDtypeStruct((run_count, rank, width), F32),
         ),
         in_specs=[
             pl.BlockSpec(memory_space=pl.ANY), vmem, vmem, vmem,
-            pl.BlockSpec(memory_space=pltpu.SMEM), vmem,
+            pl.BlockSpec(memory_space=pltpu.SMEM), vmem, vmem, vmem,
         ],
         out_specs=(vmem, vmem),
         scratch_shapes=[
             pltpu.VMEM((run_count * times, width), BF16),
-            pltpu.VMEM((run_count, rank, times), BF16),
-            pltpu.VMEM((4, per, rank, times), BF16),
+            pltpu.VMEM((run_count, rank, times), F32),
+            pltpu.VMEM((4, per, rank, times), F32),
             pltpu.VMEM((per, rank, times), F32),
             pltpu.VMEM((run_count, rank, times), BF16),
             pltpu.VMEM((n, rank, w), BF16),
@@ -292,8 +295,8 @@
             pltpu.VMEM((n, rank, w), BF16),
             pltpu.VMEM((2 * rank, width), BF16),
             pltpu.VMEM((2 * rank, run_count * times), BF16),
-            pltpu.VMEM((run_count, rank, times), BF16),
-            pltpu.VMEM((4, per, rank, times), BF16),
+            pltpu.VMEM((run_count, rank, times), F32),
+            pltpu.VMEM((4, per, rank, times), F32),
             pltpu.VMEM((per, rank, times), F32),
             pltpu.VMEM((run_count, rank, times), BF16),
             dma((run_count,)),
@@ -310,9 +313,9 @@
         name="parafac_half",
     )(
         slices, spectra.reshape(2 * rank, width), own_mix, held_mix,
-        my_halves.astype(F32), system,
+        my_halves.astype(F32), halves[:, None], loadings, mixing,
     )
-    return (new_spectra, residual)
+    return (new_spectra.astype(F32), residual)
 
 
 def solution(mesh):

time: 90.3 us -> 93.8 us (1.039)
  Pallas kernels: 74.8 us -> 79.1 us
  matrix products: 4.62 us -> 1.82 us
  other arithmetic: 2.95 us -> 4.24 us
    pallas_call x1, Pallas kernels: 74.8 us -> 79.1 us  [body(): pl.pallas_call(functools.partial(kernel, n), out_shape=(jax.ShapeDtypeStr...]
    dot_general x2 -> x0, matrix products: 2.78 us -> none  [the longest x1 1.61 us: body(): jnp.einsum('kh,kr,ks->hrs', member, loadings, loadings, precision=HI)]
    convert_element_type x0 -> x1, other arithmetic: none -> 1.95 us  [body(): return (new_spectra.astype(F32), residual)]
    broadcast_in_dim x0 -> x1, local copies, waits for them, and re-layouts: none -> 1.34 us  [body(): halves[:, None]]
where the time goes in v2:
time: 93.8 us; the launch traced here: 93.3 us
  Pallas kernels  79.1 us (84%)
  local copies, waits for them, and re-layouts  7.46 us (8%)
  other arithmetic  4.24 us (5%)
  matrix products  1.82 us (2%)
    pallas_call x1, Pallas kernels, body(): pl.pallas_call(functools.partial(kernel, n), out_shape=(jax.ShapeDtypeStr...  79.1 us
    unnamed x2, local copies, waits for them, and re-layouts  5.33 us
    convert_element_type x1, other arithmetic, body(): return (new_spectra.astype(F32), residual)  1.95 us

profile of v2, /device:TPU:11, one launch (start us, length us, event | category | flops | bytes accessed | tf_op | source)
XLA Modules:
  0.0 93.3 jit_solution(15604511494819820464)
XLA Ops:
  0.6 0.9 select_reduce_fusion
  1.5 0.9 fusion.1
  2.5 0.8 slice_bitcast_fusion.1
  3.2 0.9 fusion
  4.1 0.9 select_multiply_fusion
  5.0 0.5 convert_element_type.8.hf
  5.5 1.3 %copy.10.halves = s32[64,1]{1,0:T(8,128)} copy(s32[64,1]{0,1:T(1,128)} %bitcast.9) | data formatting | bytes 512 | tf_op jit(solution)/shard_map/broadcast_in_dim | solution.py:316
  6.9 1.4 %copy.11.loadings = f32[64,48]{1,0:T(8,128)} copy(f32[64,48]{0,1:T(8,128)} %param.8) | data formatting | bytes 24576 | tf_op args[2]
  8.3 79.1 %parafac_half.1 = (bf16[2,48,2048]{2,1,0:T(8,128)(2,1)}, f32[8,48,2048]{2,1,0:T(8,128)}) custom-call(bf16[8,512,2048]{2,1,0:T(8,128)(2,1)} %sl.1, bf16[96,2048]{1,0:T(8,128)(2,1)} %bitcast.8, f32[8,48,48]{2,1,0:T(8,128)} %get-tuple-element.9.omix, f32[8,48,48]{2,1,0:T(8,128)} %get-tuple-element.8.hmix, f32[8]{0:T(128)} %convert_element_type.8.hf, ...), custom_call_target="tpu_custom_call" | custom-call | tf_op jit(solution)/shard_map/parafac_half/pallas_call | solution.py:275
  87.4 1.9 %convert_element_type.9 = f32[2,48,2048]{2,1,0:T(8,128)} convert(bf16[2,48,2048]{2,1,0:T(8,128)(2,1)} %get-tuple-element.4) | non-fusion elementwise | flops 196608 | bytes 1179648 | tf_op jit(solution)/shard_map/convert_element_type | solution.py:318
  89.4 3.9 %copy.13 = f32[8,48,2048]{2,1,0:T(8,128)} copy(f32[8,48,2048]{2,1,0:T(8,128)} %get-tuple-element.15) | data formatting | bytes 6291456
  (2 shorter events, 0.0 us)
